TPU v7x, 32 devices: a whole 2x2x4 slice. The times are simulated.
32 devices in a mesh: grp: 8 (over z, y), seq: 4 (over x, core).
Axes of the slice: x: 2, y: 2, z: 4, core: 2. Of those that a mesh axis runs over, the one named last changes fastest.
Arguments:
- tokens_in: bfloat16 [24576, 768], P(('grp', 'seq')), may hold values from -6 to 6
- lengths: int32 [8], P('grp'), may hold values from 2305 to 3072, as said below
- ln1_gain: float32 [768], replicated, may hold values from 0.5 to 1.5
- ln1_bias: float32 [768], replicated, may hold values from -1.75 to 1.75
- w_qkv: bfloat16 [768, 2304], replicated, may hold values from -0.21875 to 0.21875
- bias_query: float32 [768], replicated, may hold values from -1.75 to 1.75
- bias_value: float32 [768], replicated, may hold values from -1.75 to 1.75
- w_out: bfloat16 [768, 768], replicated, may hold values from -0.875 to 0.875
- bias_out: float32 [768], replicated, may hold values from -1.75 to 1.75
- ln2_gain: float32 [768], replicated, may hold values from 0.5 to 1.5
- ln2_bias: float32 [768], replicated, may hold values from -1.75 to 1.75
- w_up: bfloat16 [768, 3072], replicated, may hold values from -0.21875 to 0.21875
- bias_up: float32 [3072], replicated, may hold values from -1.75 to 1.75
- w_down: bfloat16 [3072, 768], replicated, may hold values from -0.109375 to 0.109375
- bias_down: float32 [768], replicated, may hold values from -1.75 to 1.75
- proj_patch: bfloat16 [768, 768], replicated, may hold values from -0.21875 to 0.21875
- proj_class: bfloat16 [768, 768], replicated, may hold values from -0.21875 to 0.21875
- class_emb: bfloat16 [150, 768], replicated, may hold values from -6 to 6
- d_masks: bfloat16 [24576, 150], P(('grp', 'seq')), may hold values from -6 to 6
Outputs:
- masks: bfloat16 [24576, 150], P(('grp', 'seq'))
- grad_tokens: bfloat16 [24576, 768], P(('grp', 'seq'))
- grad_ln1_gain: float32 [768], P('grp')
- grad_ln1_bias: float32 [768], P('grp')
- grad_w_qkv: float32 [768, 2304], P('grp', 'seq')
- grad_bias_query: float32 [768], P('grp')
- grad_bias_value: float32 [768], P('grp')
- grad_w_out: float32 [768, 768], P('grp', 'seq')
- grad_bias_out: float32 [768], P('grp')
- grad_ln2_gain: float32 [768], P('grp')
- grad_ln2_bias: float32 [768], P('grp')
- grad_w_up: float32 [768, 3072], P('grp', 'seq')
- grad_bias_up: float32 [3072], P('grp')
- grad_w_down: float32 [3072, 768], P('grp', 'seq')
- grad_bias_down: float32 [768], P('grp')
- grad_proj_patch: float32 [768, 768], P('grp', 'seq')
- grad_proj_class: float32 [768, 768], P('grp', 'seq')
- grad_class_emb: float32 [150, 768], P(None, 'grp')
Inputs may be any that keep to these rules, and one draw needn't show every extreme that they name: Image g fills the first lengths[g] rows of its 3072 rows, the rest is padding; in every draw some image has exactly 3072 rows.
All inputs are finite; a program needn't handle non-finite values.
Results may differ from a plain program's by a relative error of at most 0.015.
Values may be sent and summed in bfloat16 or wider, within the bound.
A program may use at most 256 MiB of HBM per device.

v0:
```python
import math
import jax
import jax.numpy as jnp
from jax import lax
from jax.sharding import PartitionSpec as P

HEAD_DIM = 64
EPS_NORM = 1e-06
EPS_UNIT = 1e-06
NEG_FILL = -1e30


def layer_norm(matrix_rows, gain_vec, shift_vec):
    row_mean = jnp.mean(matrix_rows, axis=-1, keepdims=True)
    centred = matrix_rows - row_mean
    row_var = jnp.mean(centred * centred, axis=-1, keepdims=True)
    return centred * lax.rsqrt(row_var + EPS_NORM) * gain_vec + shift_vec


def unit_rows(matrix_rows):
    return matrix_rows * lax.rsqrt(
        jnp.sum(matrix_rows * matrix_rows, axis=-1, keepdims=True) + EPS_UNIT
    )


def gelu_exact(values_in):
    return jax.nn.gelu(values_in, approximate=False)


def score_block(query_heads, key_block, keep_block, score_scale):
    scores = (
        jnp.einsum("qhd,khd->hqk", query_heads, key_block, preferred_element_type=jnp.float32)
        * score_scale
    )
    return jnp.where(keep_block[None, None, :], scores, NEG_FILL)


def split_blocks(key_heads, value_heads, key_keep, key_span):
    block_count = key_heads.shape[0] // key_span
    head_count = key_heads.shape[1]
    key_blocks = key_heads.reshape(block_count, key_span, head_count, -1)
    value_blocks = value_heads.reshape(block_count, key_span, head_count, -1)
    keep_blocks = key_keep.reshape(block_count, key_span)
    return (key_blocks, value_blocks, keep_blocks)


def attend_forward(query_heads, key_heads, value_heads, key_keep, score_scale, key_span):
    row_count, head_count = (query_heads.shape[0], query_heads.shape[1])
    key_blocks, value_blocks, keep_blocks = split_blocks(key_heads, value_heads, key_keep, key_span)

    def gather_stats(carried, pieces):
        row_top, row_total = carried
        key_block, keep_block = pieces
        scores = score_block(query_heads, key_block, keep_block, score_scale)
        new_top = jnp.maximum(row_top, jnp.max(scores, axis=-1))
        row_total = row_total * jnp.exp(row_top - new_top) + jnp.sum(
            jnp.exp(scores - new_top[..., None]), axis=-1
        )
        return ((new_top, row_total), None)

    start_stats = (
        jnp.full((head_count, row_count), NEG_FILL, jnp.float32),
        jnp.zeros((head_count, row_count), jnp.float32),
    )
    row_top, row_total = lax.scan(gather_stats, start_stats, (key_blocks, keep_blocks))[0]
    log_mass = row_top + jnp.log(row_total)

    def weigh_values(summed, pieces):
        key_block, value_block, keep_block = pieces
        scores = score_block(query_heads, key_block, keep_block, score_scale)
        prob_low = jnp.exp(scores - log_mass[..., None]).astype(jnp.bfloat16)
        summed = summed + jnp.einsum(
            "hqk,khd->qhd", prob_low, value_block, preferred_element_type=jnp.float32
        )
        return (summed, None)

    start_sum = jnp.zeros(query_heads.shape, jnp.float32)
    attended = lax.scan(weigh_values, start_sum, (key_blocks, value_blocks, keep_blocks))[0]
    return (attended, log_mass)


def attend_backward(
    query_heads,
    key_heads,
    value_heads,
    key_keep,
    grad_heads,
    log_mass,
    attended,
    score_scale,
    key_span,
):
    head_count = query_heads.shape[1]
    key_blocks, value_blocks, keep_blocks = split_blocks(key_heads, value_heads, key_keep, key_span)
    row_delta = jnp.einsum("qhd,qhd->hq", grad_heads.astype(jnp.float32), attended)

    def spread_grads(grad_query, pieces):
        key_block, value_block, keep_block = pieces
        prob_rows = jnp.exp(
            score_block(query_heads, key_block, keep_block, score_scale) - log_mass[..., None]
        )
        grad_probs = jnp.einsum(
            "qhd,khd->hqk", grad_heads, value_block, preferred_element_type=jnp.float32
        )
        grad_scores = (prob_rows * (grad_probs - row_delta[..., None])).astype(jnp.bfloat16)
        grad_query = grad_query + jnp.einsum(
            "hqk,khd->qhd", grad_scores, key_block, preferred_element_type=jnp.float32
        )
        grad_key_block = (
            jnp.einsum("hqk,qhd->khd", grad_scores, query_heads, preferred_element_type=jnp.float32)
            * score_scale
        )
        grad_value_block = jnp.einsum(
            "hqk,qhd->khd",
            prob_rows.astype(jnp.bfloat16),
            grad_heads,
            preferred_element_type=jnp.float32,
        )
        return (grad_query, (grad_key_block, grad_value_block))

    start_query = jnp.zeros(query_heads.shape, jnp.float32)
    grad_query, block_grads = lax.scan(
        spread_grads, start_query, (key_blocks, value_blocks, keep_blocks)
    )
    total_rows = key_heads.shape[0]
    model_width = head_count * query_heads.shape[2]
    grad_key_all = block_grads[0].reshape(total_rows, model_width)
    grad_value_all = block_grads[1].reshape(total_rows, model_width)
    return (grad_query * score_scale, grad_key_all, grad_value_all)


def column_sum(matrix_low):
    return jnp.sum(matrix_low.astype(jnp.float32), axis=0)


def body(
    tokens_in,
    lengths,
    ln1_gain,
    ln1_bias,
    w_qkv,
    bias_query,
    bias_value,
    w_out,
    bias_out,
    ln2_gain,
    ln2_bias,
    w_up,
    bias_up,
    w_down,
    bias_down,
    proj_patch,
    proj_class,
    class_emb,
    d_masks,
):
    row_count, model_width = tokens_in.shape
    head_size = HEAD_DIM
    head_count = model_width // head_size
    seq_devices = lax.axis_size("seq")
    grp_devices = lax.axis_size("grp")
    seq_total = row_count * seq_devices
    key_span = min(512, seq_total)
    score_scale = head_size ** (-0.5)
    mask_scale = math.sqrt(model_width)
    length_here = lengths[0]
    first_row = lax.axis_index("seq") * row_count
    valid_rows = (first_row + jnp.arange(row_count, dtype=jnp.int32) < length_here).astype(
        jnp.float32
    )
    key_keep = jnp.arange(seq_total, dtype=jnp.int32) < length_here
    tokens = tokens_in.astype(jnp.float32)
    normed_one, norm_one_back = jax.vjp(layer_norm, tokens, ln1_gain, ln1_bias)
    normed_low = normed_one.astype(jnp.bfloat16)
    zero_keys = jnp.zeros_like(bias_query)
    mixed = jnp.dot(normed_low, w_qkv, preferred_element_type=jnp.float32)
    mixed = mixed + jnp.concatenate([bias_query, zero_keys, bias_value])
    mixed_low = mixed.astype(jnp.bfloat16)
    query_heads = mixed_low[:, :model_width].reshape(row_count, head_count, head_size)
    key_rows = mixed_low[:, model_width : 2 * model_width]
    value_rows = mixed_low[:, 2 * model_width :]
    key_all, value_all = (
        lax.all_gather(key_rows, "seq", axis=0, tiled=True),
        lax.all_gather(value_rows, "seq", axis=0, tiled=True),
    )
    key_heads = key_all.reshape(seq_total, head_count, head_size)
    value_heads = value_all.reshape(seq_total, head_count, head_size)
    attended, log_mass = attend_forward(
        query_heads, key_heads, value_heads, key_keep, score_scale, key_span
    )
    attended_low = attended.reshape(row_count, model_width).astype(jnp.bfloat16)
    branch = jnp.dot(attended_low, w_out, preferred_element_type=jnp.float32) + bias_out
    middle = tokens + branch
    normed_two, norm_two_back = jax.vjp(layer_norm, middle, ln2_gain, ln2_bias)
    normed_two_low = normed_two.astype(jnp.bfloat16)
    hidden = jnp.dot(normed_two_low, w_up, preferred_element_type=jnp.float32) + bias_up
    active, gelu_back = jax.vjp(gelu_exact, hidden)
    active_low = active.astype(jnp.bfloat16)
    final = middle + (jnp.dot(active_low, w_down, preferred_element_type=jnp.float32) + bias_down)
    final_low = final.astype(jnp.bfloat16)
    patches = jnp.dot(final_low, proj_patch, preferred_element_type=jnp.float32)
    patch_unit, patch_back = jax.vjp(unit_rows, patches)
    patch_low = patch_unit.astype(jnp.bfloat16)
    classes = jnp.dot(class_emb, proj_class, preferred_element_type=jnp.float32)
    class_unit, class_back = jax.vjp(unit_rows, classes)
    class_low = class_unit.astype(jnp.bfloat16)
    mask_out = jnp.einsum("rd,cd->rc", patch_low, class_low, preferred_element_type=jnp.float32)
    mask_out = (mask_out * mask_scale * valid_rows[:, None]).astype(jnp.bfloat16)
    mask_grad = (d_masks.astype(jnp.float32) * valid_rows[:, None]).astype(jnp.bfloat16)
    grad_patch_unit = jnp.dot(mask_grad, class_low, preferred_element_type=jnp.float32) * mask_scale
    class_part = (
        jnp.einsum("rc,rd->cd", mask_grad, patch_low, preferred_element_type=jnp.float32)
        * mask_scale
    )
    class_total = lax.psum(class_part, ("grp", "seq"))
    grad_classes = class_back(class_total)[0].astype(jnp.bfloat16)
    class_proj_full = jnp.einsum(
        "cd,ce->de", class_emb, grad_classes, preferred_element_type=jnp.float32
    )
    class_emb_full = jnp.einsum(
        "ce,de->cd", grad_classes, proj_class, preferred_element_type=jnp.float32
    )
    grad_patches = patch_back(grad_patch_unit)[0].astype(jnp.bfloat16)
    grad_proj_patch = jnp.einsum(
        "rd,re->de", final_low, grad_patches, preferred_element_type=jnp.float32
    )
    grad_final = jnp.einsum(
        "re,de->rd", grad_patches, proj_patch, preferred_element_type=jnp.float32
    )
    grad_feed = grad_final.astype(jnp.bfloat16)
    grad_w_down = jnp.einsum("rf,rd->fd", active_low, grad_feed, preferred_element_type=jnp.float32)
    grad_bias_down = column_sum(grad_feed)
    grad_active = jnp.einsum("rd,fd->rf", grad_feed, w_down, preferred_element_type=jnp.float32)
    grad_hidden = gelu_back(grad_active)[0].astype(jnp.bfloat16)
    grad_w_up = jnp.einsum(
        "rd,rf->df", normed_two_low, grad_hidden, preferred_element_type=jnp.float32
    )
    grad_bias_up = column_sum(grad_hidden)
    grad_normed_two = jnp.einsum("rf,df->rd", grad_hidden, w_up, preferred_element_type=jnp.float32)
    grad_middle_norm, grad_ln2_gain, grad_ln2_bias = norm_two_back(grad_normed_two)
    grad_middle = grad_final + grad_middle_norm
    grad_branch = grad_middle.astype(jnp.bfloat16)
    grad_w_out = jnp.einsum(
        "rd,re->de", attended_low, grad_branch, preferred_element_type=jnp.float32
    )
    grad_bias_out = column_sum(grad_branch)
    grad_attended = jnp.einsum("re,de->rd", grad_branch, w_out, preferred_element_type=jnp.float32)
    grad_heads = grad_attended.astype(jnp.bfloat16).reshape(row_count, head_count, head_size)
    grad_query, grad_key_all, grad_value_all = attend_backward(
        query_heads,
        key_heads,
        value_heads,
        key_keep,
        grad_heads,
        log_mass,
        attended,
        score_scale,
        key_span,
    )
    grad_key_own, grad_value_own = (
        lax.psum_scatter(
            grad_key_all.astype(jnp.bfloat16), "seq", scatter_dimension=0, tiled=True
        ).astype(jnp.float32),
        lax.psum_scatter(
            grad_value_all.astype(jnp.bfloat16), "seq", scatter_dimension=0, tiled=True
        ).astype(jnp.float32),
    )
    grad_mixed = jnp.concatenate(
        [grad_query.reshape(row_count, model_width), grad_key_own, grad_value_own], axis=1
    ).astype(jnp.bfloat16)
    grad_w_qkv = jnp.einsum("rd,rm->dm", normed_low, grad_mixed, preferred_element_type=jnp.float32)
    grad_bias_all = column_sum(grad_mixed)
    grad_bias_query = grad_bias_all[:model_width]
    grad_bias_value = grad_bias_all[2 * model_width :]
    grad_normed_one = jnp.einsum("rm,dm->rd", grad_mixed, w_qkv, preferred_element_type=jnp.float32)
    grad_tokens_norm, grad_ln1_gain, grad_ln1_bias = norm_one_back(grad_normed_one)
    grad_tokens = (grad_middle + grad_tokens_norm).astype(jnp.bfloat16)
    row_parts = (
        lax.psum_scatter(grad_w_qkv, "grp", scatter_dimension=0, tiled=True),
        lax.psum_scatter(grad_w_out, "grp", scatter_dimension=0, tiled=True),
        lax.psum_scatter(grad_w_up, "grp", scatter_dimension=0, tiled=True),
        lax.psum_scatter(grad_w_down, "grp", scatter_dimension=0, tiled=True),
        lax.psum_scatter(grad_proj_patch, "grp", scatter_dimension=0, tiled=True),
        lax.psum_scatter(grad_ln1_gain, "grp", scatter_dimension=0, tiled=True),
        lax.psum_scatter(grad_ln1_bias, "grp", scatter_dimension=0, tiled=True),
        lax.psum_scatter(grad_bias_query, "grp", scatter_dimension=0, tiled=True),
        lax.psum_scatter(grad_bias_value, "grp", scatter_dimension=0, tiled=True),
        lax.psum_scatter(grad_bias_out, "grp", scatter_dimension=0, tiled=True),
        lax.psum_scatter(grad_ln2_gain, "grp", scatter_dimension=0, tiled=True),
        lax.psum_scatter(grad_ln2_bias, "grp", scatter_dimension=0, tiled=True),
        lax.psum_scatter(grad_bias_up, "grp", scatter_dimension=0, tiled=True),
        lax.psum_scatter(grad_bias_down, "grp", scatter_dimension=0, tiled=True),
    )
    matrix_parts = (
        lax.psum_scatter(
            row_parts[0].astype(jnp.bfloat16), "seq", scatter_dimension=1, tiled=True
        ).astype(jnp.float32),
        lax.psum_scatter(
            row_parts[1].astype(jnp.bfloat16), "seq", scatter_dimension=1, tiled=True
        ).astype(jnp.float32),
        lax.psum_scatter(
            row_parts[2].astype(jnp.bfloat16), "seq", scatter_dimension=1, tiled=True
        ).astype(jnp.float32),
        lax.psum_scatter(
            row_parts[3].astype(jnp.bfloat16), "seq", scatter_dimension=1, tiled=True
        ).astype(jnp.float32),
        lax.psum_scatter(
            row_parts[4].astype(jnp.bfloat16), "seq", scatter_dimension=1, tiled=True
        ).astype(jnp.float32),
    )
    vector_parts = lax.psum(
        (
            row_parts[5],
            row_parts[6],
            row_parts[7],
            row_parts[8],
            row_parts[9],
            row_parts[10],
            row_parts[11],
            row_parts[12],
            row_parts[13],
        ),
        "seq",
    )
    rows_each = model_width // grp_devices
    cols_each = model_width // seq_devices
    grp_here = lax.axis_index("grp")
    seq_here = lax.axis_index("seq")
    grad_proj_class = lax.dynamic_slice(
        class_proj_full, (grp_here * rows_each, seq_here * cols_each), (rows_each, cols_each)
    )
    grad_class_emb = lax.dynamic_slice_in_dim(class_emb_full, grp_here * rows_each, rows_each, 1)
    return (
        mask_out,
        grad_tokens,
        vector_parts[0],
        vector_parts[1],
        matrix_parts[0],
        vector_parts[2],
        vector_parts[3],
        matrix_parts[1],
        vector_parts[4],
        vector_parts[5],
        vector_parts[6],
        matrix_parts[2],
        vector_parts[7],
        matrix_parts[3],
        vector_parts[8],
        matrix_parts[4],
        grad_proj_class,
        grad_class_emb,
    )


def solution(mesh):
    return jax.shard_map(
        body,
        mesh=mesh,
        in_specs=(
            P(("grp", "seq"), None),
            P("grp"),
            P(),
            P(),
            P(),
            P(),
            P(),
            P(),
            P(),
            P(),
            P(),
            P(),
            P(),
            P(),
            P(),
            P(),
            P(),
            P(),
            P(("grp", "seq"), None),
        ),
        out_specs=(
            P(("grp", "seq"), None),
            P(("grp", "seq"), None),
            P("grp"),
            P("grp"),
            P("grp", "seq"),
            P("grp"),
            P("grp"),
            P("grp", "seq"),
            P("grp"),
            P("grp"),
            P("grp"),
            P("grp", "seq"),
            P("grp"),
            P("grp", "seq"),
            P("grp"),
            P("grp", "seq"),
            P("grp", "seq"),
            P(None, "grp"),
        ),
        check_vma=False,
    )
```

profile of v0, /device:TPU:0, one launch (start us, length us, event | category | flops | bytes accessed | tf_op | source)
XLA Modules:
  0.0 1562.4 jit_solution(7666178320111044407)
XLA Ops:
  30.2 29.2 %all-gather.5.cloned.1.call-done = bf16[3072,768]{1,0:T(8,128)(2,1)} async-done(((bf16[768,768]{1,0:T(8,128)(2,1)}), bf16[3072,768]{1,0:T(8,128)(2,1)}) %all-gather.5.cloned.1.call-update) | async-done | bytes 4718608 | tf_op jit(solution)/shard_map/all_gather | solution.py:183
  59.4 15.0 reshape.189
  74.4 13.5 copy.80
  88.0 165.2 %while.39 = (s32[]{:T(128)}, f32[12,768]{1,0:T(8,128)}, f32[12,768]{1,0:T(8,128)}, pred[6,512]{1,0:T(8,128)(4,1)S(1)}, bf16[6,512,12,64]{1,3,2,0:T(8,128)(2,1)},...) while((s32[]{:T(128)}, f32[12,768]{1,0:T(8,128)}, f32[12,768]{1,0:T(8,128)}, ...), condition=%wide.region_5.6_spmd.clone, body=%wide.region_2.5_spmd.clone.sunk | while | flops 637056000 | bytes 40196704 | solution.py:65
  88.0 12.4 bitcast_reduce_fusion.2
  101.8 10.8 fusion.145
  115.5 12.3 bitcast_reduce_fusion.2
  129.3 10.8 fusion.145
  143.0 12.3 bitcast_reduce_fusion.2
  156.8 10.8 fusion.145
  170.6 12.3 bitcast_reduce_fusion.2
  184.3 10.8 fusion.145
  198.1 12.3 bitcast_reduce_fusion.2
  211.9 10.8 fusion.145
  225.6 12.3 bitcast_reduce_fusion.2
  239.4 10.8 fusion.145
  253.2 15.0 reshape.188
  268.1 13.6 copy.79
  283.2 61.1 %while.40 = (s32[]{:T(128)}, f32[768,12,64]{0,2,1:T(8,128)}, bf16[6,512,12,64]{1,3,2,0:T(8,128)(2,1)}, pred[6,512]{1,0:T(8,128)(4,1)S(1)}, bf16[6,512,12,64]{1,3...) while((s32[]{:T(128)}, f32[768,12,64]{0,2,1:T(8,128)}, ...), condition=%wide.region_7.8_spmd.clone, body=%wide.region_6.7_spmd.clone.sunk | while | flops 1228013568 | bytes 7522923 | solution.py:78
  350.3 28.6 %multiply_convert_fusion.1 = (bf16[768,3072]{1,0:T(8,128)(2,1)S(1)}, f32[768,3072]{1,0:T(8,128)}, f32[768,3072]{1,0:T(8,128)}) fusion(f32[3072]{0:T(1024)S(1)} %copy-done.54, bf16[768,3072]{1,0:T(8,128)(2,1)S(1)} %bitcast.171, f32[768,768]{0,1:T(8,128)S(1)} %get-tuple-element.449, f32[768]{0:T(1024)S(1)} %copy-done.57, f32[768]{0:T(1024)S(1)} %copy-done.42, ...), kind=kOutput, calls=%fused_computation.51 | convolution fusion | flops 3782541312 | bytes 30695424 | tf_op jit(solution)/shard_map/dot_general | solution.py:196
  395.1 13.0 convert_reduce_fusion
  433.9 291.4 %while.41 = (s32[]{:T(128)}, f32[768,12,64]{0,2,1:T(8,128)}, bf16[6,512,12,64]{1,3,2,0:T(8,128)(2,1)}, bf16[6,512,12,64]{1,3,2,0:T(8,128)(2,1)}, bf16[6,512,12,6...) while((s32[]{:T(128)}, f32[768,12,64]{0,2,1:T(8,128)}, ...), condition=%wide.region_16.17_spmd.clone, body=%wide.region_15.16_spmd.clone.sunk | while | flops 3068657664 | bytes 142766832 | solution.py:122
  434.4 10.6 fusion.160
  445.0 10.9 multiply_convert_fusion.13
  470.6 11.9 bitcast_dynamic-update-slice_fusion.5
  482.5 10.6 fusion.160
  493.2 10.8 multiply_convert_fusion.13
  519.2 11.9 bitcast_dynamic-update-slice_fusion.5
  531.1 10.6 fusion.160
  541.8 10.7 multiply_convert_fusion.13
  567.8 11.9 bitcast_dynamic-update-slice_fusion.5
  590.4 10.7 multiply_convert_fusion.13
  616.3 11.9 bitcast_dynamic-update-slice_fusion.5
  628.2 10.6 fusion.160
  638.8 10.7 multiply_convert_fusion.13
  664.8 11.9 bitcast_dynamic-update-slice_fusion.5
  676.7 10.6 fusion.160
  687.3 10.7 multiply_convert_fusion.13
  713.3 11.8 bitcast_dynamic-update-slice_fusion.5
  751.4 10.7 fusion.67
  769.3 10.7 fusion.77
  784.4 50.4 %reduce-scatter.23.cloned.1.call-done = bf16[768,768]{0,1:T(8,128)(2,1)} async-done(((bf16[3072,768]{0,1:T(8,128)(2,1)}), bf16[768,768]{0,1:T(8,128)(2,1)}) %reduce-scatter.23.cloned.1.call-update) | async-done | bytes 1179664 | tf_op jit(solution)/shard_map/reduce_scatter | solution.py:264
  848.8 118.0 %all-reduce.13.cloned.1.call-done = f32[150,768]{1,0:T(8,128)} async-done(((f32[150,768]{1,0:T(8,128)}), f32[150,768]{1,0:T(8,128)}) %all-reduce.13.cloned.1.call-update) | async-done | bytes 460816 | tf_op jit(solution)/shard_map/psum | solution.py:215
  968.6 165.9 %reduce-scatter.33.cloned.1.call-done = f32[384,768]{1,0:T(8,128)} async-done(((f32[3072,768]{1,0:T(8,128)}), f32[384,768]{1,0:T(8,128)}) %reduce-scatter.33.cloned.1.call-update) | async-done | bytes 1179664 | tf_op jit(solution)/shard_map/reduce_scatter | solution.py:282
  1159.6 19.8 %reduce-scatter.39.cloned.1.call-done = bf16[192,96]{1,0:T(8,128)(2,1)} async-done(((bf16[768,96]{1,0:T(8,128)(2,1)}), bf16[192,96]{1,0:T(8,128)(2,1)}) %reduce-scatter.39.cloned.1.call-update) | async-done | bytes 36880
  1182.3 164.4 %reduce-scatter.29.cloned.1.call-done = f32[96,3072]{1,0:T(8,128)} async-done(((f32[768,3072]{1,0:T(8,128)}), f32[96,3072]{1,0:T(8,128)}) %reduce-scatter.29.cloned.1.call-update) | async-done | bytes 1179664 | tf_op jit(solution)/shard_map/reduce_scatter | solution.py:281
  1366.1 112.8 %reduce-scatter.25.cloned.1.call-done = f32[96,2304]{1,0:T(8,128)} async-done(((f32[768,2304]{1,0:T(8,128)}), f32[96,2304]{1,0:T(8,128)}) %reduce-scatter.25.cloned.1.call-update) | async-done | bytes 884752 | tf_op jit(solution)/shard_map/reduce_scatter | solution.py:279
  1484.3 36.8 %all-reduce.9 = (f32[768]{0:T(1024)}, f32[768]{0:T(1024)}, f32[768]{0:T(1024)}, f32[768]{0:T(1024)}, f32[768]{0:T(1024)}, /*index=5*/f32[768]{0:T(1024)}, f32[768]{0:T(1024)}, f32[3072]{0:T(1024)}, f32[768]{0:T(1024)}) all-reduce(f32[768]{0:T(1024)} %get-tuple-element.362, ...), channel_id=4, replica_groups=mesh['grp'=8,'seq'=4] {'grp'}, use_global_device_ids=true, to_apply=%region_22.23.clone | all-reduce | flops 9216 | bytes 73728
  (365 shorter events, 399.1 us)
Async XLA Ops:
  7.2 52.1 %all-gather.5.cloned.1.call-start = ((), (), s32[]{:S(2)}) async-start(), calls=%async_computation.13 | async-start | bytes 5898240 | tf_op jit(solution)/shard_map/all_gather | solution.py:183
  19.1 234.1 %all-gather.3.cloned.1.call-start = ((), (), s32[]{:S(2)}) async-start(), calls=%async_computation.12 | async-start | bytes 5898240 | tf_op jit(solution)/shard_map/all_gather | solution.py:184
  19.8 742.3 %reduce-scatter.35.cloned.1.call-start = ((), (), s32[]{:S(2)}) async-start(), calls=%async_computation.21 | async-start | bytes 2654208 | tf_op jit(solution)/shard_map/reduce_scatter | solution.py:283
  26.3 48.1 %copy-start.40 = (f32[150]{0:T(256)}, f32[150]{0:T(256)S(1)}, u32[]{:S(2)}) copy-start(f32[150]{0:T(256)S(1)} %add_rsqrt_fusion.1) | copy-start | bytes 1804
  346.6 32.3 %slice-start = ((s8[4718592]{0:T(1024)(128)(4,1)}), s8[4194304]{0:T(1024)(128)(4,1)S(1)}, s32[]{:S(2)}) async-start(s8[4718592]{0:T(1024)(128)(4,1)} %bitcast.168), calls=%async_computation.27 | async-start | bytes 8388608
  347.9 31.0 %copy-start.7 = (f32[768,768]{0,1:T(8,128)}, f32[768,768]{0,1:T(8,128)S(1)}, u32[]{:S(2)}) copy-start(f32[768,768]{0,1:T(8,128)S(1)} %get-tuple-element.449) | copy-start | bytes 7077892
  348.0 77.0 %copy-start.24 = (f32[768]{0:T(1024)}, f32[768]{0:T(1024)S(1)}, u32[]{:S(2)}) copy-start(f32[768]{0:T(1024)S(1)} %broadcast_multiply_fusion.1) | copy-start | bytes 9220
  350.3 74.7 %copy-start.38 = (f32[768]{0:T(1024)}, f32[768]{0:T(1024)S(1)}, u32[]{:S(2)}) copy-start(f32[768]{0:T(1024)S(1)} %fusion.66) | copy-start | bytes 9220
  350.3 28.7 %slice-start.1 = ((s8[4718592]{0:T(1024)(128)(4,1)}), s8[524288]{0:T(1024)(128)(4,1)S(1)}, s32[]{:S(2)}) async-start(s8[4718592]{0:T(1024)(128)(4,1)} %bitcast.168), calls=%async_computation.28 | async-start | bytes 1048576
  350.3 28.7 %copy-start.56 = (f32[768]{0:T(1024)S(1)}, f32[768]{0:T(1024)}, u32[]{:S(2)}) copy-start(f32[768]{0:T(1024)} %param.39) | copy-start | bytes 9220
  391.7 373.9 %reduce-scatter.27.cloned.1.call-start = ((), (), s32[]{:S(2)}) async-start(), calls=%async_computation.17 | async-start | bytes 2654208 | tf_op jit(solution)/shard_map/reduce_scatter | solution.py:280
  408.1 9.9 copy-start.60
  433.8 350.6 %reduce-scatter.21.cloned.1.call-start = ((), (), s32[]{:S(2)}) async-start(), calls=%async_computation.14 | async-start | bytes 5898240 | tf_op jit(solution)/shard_map/reduce_scatter | solution.py:261
  434.3 10.7 copy-start.26
  434.3 10.7 copy-start.27
  445.0 14.6 copy-start.2
  482.5 10.7 copy-start.26
  482.5 10.7 copy-start.27
  493.2 14.5 copy-start.2
  531.1 10.7 copy-start.26
  531.1 10.7 copy-start.27
  541.8 14.4 copy-start.2
  579.7 10.7 copy-start.26
  579.7 10.7 copy-start.27
  590.4 14.4 copy-start.2
  628.2 10.7 copy-start.26
  628.2 10.7 copy-start.27
  638.8 14.4 copy-start.2
  676.7 10.7 copy-start.26
  676.7 10.7 copy-start.27
  687.3 14.4 copy-start.2
  736.2 98.6 %reduce-scatter.23.cloned.1.call-start = ((), (), s32[]{:S(2)}) async-start(), calls=%async_computation.15 | async-start | bytes 5898240 | tf_op jit(solution)/shard_map/reduce_scatter | solution.py:264
  747.4 219.4 %all-reduce.13.cloned.1.call-start = ((), (), s32[]{:S(2)}) async-start(), calls=%async_computation.22 | async-start | bytes 933888 | tf_op jit(solution)/shard_map/psum | solution.py:215
  751.3 383.3 %reduce-scatter.33.cloned.1.call-start = ((), (), s32[]{:S(2)}) async-start(), calls=%async_computation.20 | async-start | bytes 10616832 | tf_op jit(solution)/shard_map/reduce_scatter | solution.py:282
  762.0 7.2 copy-start.25
  762.0 7.2 copy-start.39
  762.0 7.2 copy-start.44
  762.0 394.6 %reduce-scatter.43.cloned.1.call-start = ((), (), s32[]{:S(2)}) async-start(), calls=%async_computation.26 | async-start | bytes 245760
  765.5 413.9 %reduce-scatter.39.cloned.1.call-start = ((), (), s32[]{:S(2)}) async-start(), calls=%async_computation.24 | async-start | bytes 245760
  769.0 577.8 %reduce-scatter.29.cloned.1.call-start = ((), (), s32[]{:S(2)}) async-start(), calls=%async_computation.18 | async-start | bytes 10616832 | tf_op jit(solution)/shard_map/reduce_scatter | solution.py:281
  780.0 54.9 %copy-start.23 = (f32[768]{0:T(1024)S(1)}, f32[768]{0:T(1024)}, u32[]{:S(2)}) copy-start(f32[768]{0:T(1024)} %copy-done.22) | copy-start | bytes 9220
  780.0 54.9 %copy-start.32 = (f32[768]{0:T(1024)S(1)}, f32[768]{0:T(1024)}, u32[]{:S(2)}) copy-start(f32[768]{0:T(1024)} %copy-done.31) | copy-start | bytes 9220
  780.0 54.9 %copy-start.36 = (f32[768]{0:T(1024)S(1)}, f32[768]{0:T(1024)}, u32[]{:S(2)}) copy-start(f32[768]{0:T(1024)} %param.27) | copy-start | bytes 9220
  780.0 698.9 %reduce-scatter.25.cloned.1.call-start = ((), (), s32[]{:S(2)}) async-start(), calls=%async_computation.16 | async-start | bytes 7962624 | tf_op jit(solution)/shard_map/reduce_scatter | solution.py:279
  843.3 703.7 %reduce-scatter.41.cloned.1.call-start = ((), (), s32[]{:S(2)}) async-start(), calls=%async_computation.25 | async-start | bytes 737280
  848.8 290.8 %copy-start.41 = (f32[150]{0:T(256)S(1)}, f32[150]{0:T(256)}, u32[]{:S(2)}) copy-start(f32[150]{0:T(256)} %copy-done.40) | copy-start | bytes 1804
  1138.9 411.6 %reduce-scatter.31.cloned.1.call-start = ((), (), s32[]{:S(2)}) async-start(), calls=%async_computation.19 | async-start | bytes 737280 | tf_op jit(solution)/shard_map/reduce_scatter | solution.py:301
  1348.9 203.2 %reduce-scatter.37.cloned.1.call-start = ((), (), s32[]{:S(2)}) async-start(), calls=%async_computation.23 | async-start | bytes 737280
  (52 other events, 155.8 us)
Sparse Core Ops, SparseCore 0:
  19.2 40.1 all-gather.4
  60.9 37.4 all-gather.2
  391.8 69.1 reduce-scatter.34
  464.4 68.0 reduce-scatter.26
  736.4 48.0 reduce-scatter.20
  787.0 47.8 reduce-scatter.22
  840.2 126.5 all-reduce.12
  970.8 163.7 reduce-scatter.32
  1137.7 18.8 reduce-scatter.42
  1159.6 19.7 reduce-scatter.38
  1183.4 163.2 reduce-scatter.28
  1350.7 128.1 reduce-scatter.24
  1481.4 21.1 reduce-scatter.40
  1504.9 22.0 reduce-scatter.30
  1529.4 22.0 reduce-scatter.36
where the time goes:
time: 1570 us; the launch traced here: 1560 us
  waiting for transfers between devices  671 us (43%)
  matrix products  526 us (34%)
  local copies, waits for them, and re-layouts  171 us (11%)
  other arithmetic  131 us (8%)
  blocking collectives  43.3 us (3%)
  between operations  17.1 us (1%)
    reduce_scatter x1, waiting for transfers between devices, body(): lax.psum_scatter(grad_w_down, 'grp', scatter_dimension=0, tiled=True)  166 us
    reduce_scatter x1, waiting for transfers between devices, body(): lax.psum_scatter(grad_w_up, 'grp', scatter_dimension=0, tiled=True)  164 us
    dot_general x12, matrix products, score_block(): jnp.einsum('qhd,khd->hqk', query_heads, key_block, preferred_element_type...  138 us
    psum x1, waiting for transfers between devices, body(): class_total = lax.psum(class_part, ('grp', 'seq'))  118 us
    reduce_scatter x1, waiting for transfers between devices, body(): lax.psum_scatter(grad_w_qkv, 'grp', scatter_dimension=0, tiled=True)  113 us
    unnamed x148, local copies, waits for them, and re-layouts  81.5 us
    dot_general x6, matrix products, spread_grads(): jnp.einsum('hqk,qhd->khd', prob_rows.astype(jnp.bfloat16), grad_heads, pr...  71.3 us
    reduce_sum x6, other arithmetic, gather_stats(): jnp.sum(jnp.exp(scores - new_top[..., None]), axis=-1)  64.9 us
  transfers between devices with their start and end apart: 15, of which 9 were waited for; matrix products, arithmetic and copies ran while one was open for 41% of the time, Pallas kernels for 0%

commit v1 on v0

--- a/solution.py
+++ b/solution.py
@@ -212,7 +212,7 @@
         jnp.einsum("rc,rd->cd", mask_grad, patch_low, preferred_element_type=jnp.float32)
         * mask_scale
     )
-    class_total = lax.psum(class_part, ("grp", "seq"))
+    class_total = jnp.sum(lax.all_gather(class_part, ("grp", "seq")), axis=0)
     grad_classes = class_back(class_total)[0].astype(jnp.bfloat16)
     class_proj_full = jnp.einsum(
         "cd,ce->de", class_emb, grad_classes, preferred_element_type=jnp.float32

time: 1570 us -> 1700 us (1.083)
  waiting for transfers between devices: 671 us -> 791 us
    psum x1 -> x0, waiting for transfers between devices: 118 us -> none  [body(): class_total = lax.psum(class_part, ('grp', 'seq'))]
    all_gather x0 -> x1, waiting for transfers between devices: none -> 92.5 us  [body(): class_total = jnp.sum(lax.all_gather(class_part, ('grp', 'seq')), axis=0)]
    reduce_scatter x1, waiting for transfers between devices: 0.02 us -> 68 us  [body(): lax.psum_scatter(grad_w_out, 'grp', scatter_dimension=0, tiled=True)]
    reduce_scatter x1, waiting for transfers between devices: 0.02 us -> 64.1 us  [body(): lax.psum_scatter(grad_proj_patch, 'grp', scatter_dimension=0, tiled=True)]
    unnamed x148 -> x156, local copies, waits for them, and re-layouts: 81.5 us -> 80 us
  transfers between devices with their start and end apart: 15 -> 15, of which waited for: 9 -> 11; matrix products, arithmetic and copies ran while one was open for 41% -> 19% of each run, Pallas kernels for 0% -> 0%
where the time goes in v1:
time: 1700 us; the launch traced here: 1690 us
  waiting for transfers between devices  791 us (47%)
  matrix products  528 us (31%)
  local copies, waits for them, and re-layouts  169 us (10%)
  other arithmetic  136 us (8%)
  blocking collectives  45.2 us (3%)
  between operations  17 us (1%)
    reduce_scatter x1, waiting for transfers between devices, body(): lax.psum_scatter(grad_w_down, 'grp', scatter_dimension=0, tiled=True)  163 us
    reduce_scatter x1, waiting for transfers between devices, body(): lax.psum_scatter(grad_w_up, 'grp', scatter_dimension=0, tiled=True)  162 us
    dot_general x12, matrix products, score_block(): jnp.einsum('qhd,khd->hqk', query_heads, key_block, preferred_element_type...  138 us
    reduce_scatter x1, waiting for transfers between devices, body(): lax.psum_scatter(grad_w_qkv, 'grp', scatter_dimension=0, tiled=True)  130 us
    all_gather x1, waiting for transfers between devices, body(): class_total = jnp.sum(lax.all_gather(class_part, ('grp', 'seq')), axis=0)  92.5 us
    unnamed x156, local copies, waits for them, and re-layouts  80 us
    dot_general x6, matrix products, spread_grads(): jnp.einsum('hqk,qhd->khd', prob_rows.astype(jnp.bfloat16), grad_heads, pr...  71.2 us
    reduce_scatter x1, waiting for transfers between devices, body(): lax.psum_scatter(grad_w_out, 'grp', scatter_dimension=0, tiled=True)  68 us
  transfers between devices with their start and end apart: 15, of which 11 were waited for; matrix products, arithmetic and copies ran while one was open for 19% of the time, Pallas kernels for 0%

profile of v1, /device:TPU:0, one launch (start us, length us, event | category | flops | bytes accessed | tf_op | source)
XLA Modules:
  0.0 1688.4 jit_solution(727994105951766784)
XLA Ops:
  30.1 29.3 %all-gather.8.cloned.1.call-done = bf16[3072,768]{1,0:T(8,128)(2,1)} async-done(((bf16[768,768]{1,0:T(8,128)(2,1)}), bf16[3072,768]{1,0:T(8,128)(2,1)}) %all-gather.8.cloned.1.call-update) | async-done | bytes 4718608 | tf_op jit(solution)/shard_map/all_gather | solution.py:183
  59.4 15.1 reshape.193
  74.4 13.5 copy.80
  88.0 165.2 %while.39 = (s32[]{:T(128)}, f32[12,768]{1,0:T(8,128)}, f32[12,768]{1,0:T(8,128)}, pred[6,512]{1,0:T(8,128)(4,1)S(1)}, bf16[6,512,12,64]{1,3,2,0:T(8,128)(2,1)},...) while((s32[]{:T(128)}, f32[12,768]{1,0:T(8,128)}, f32[12,768]{1,0:T(8,128)}, ...), condition=%wide.region_5.6_spmd.clone, body=%wide.region_2.5_spmd.clone.sunk | while | flops 637056000 | bytes 40196704 | solution.py:65
  88.0 12.3 bitcast_reduce_fusion.2
  101.8 10.8 fusion.146
  115.5 12.3 bitcast_reduce_fusion.2
  129.3 10.8 fusion.146
  143.0 12.3 bitcast_reduce_fusion.2
  156.8 10.8 fusion.146
  170.6 12.3 bitcast_reduce_fusion.2
  184.3 10.8 fusion.146
  198.1 12.3 bitcast_reduce_fusion.2
  211.9 10.8 fusion.146
  225.7 12.3 bitcast_reduce_fusion.2
  239.4 10.8 fusion.146
  253.2 15.0 reshape.192
  268.2 13.6 copy.79
  283.2 61.5 %while.40 = (s32[]{:T(128)}, f32[768,12,64]{0,2,1:T(8,128)}, bf16[6,512,12,64]{1,3,2,0:T(8,128)(2,1)}, pred[6,512]{1,0:T(8,128)(4,1)S(1)}, bf16[6,512,12,64]{1,3...) while((s32[]{:T(128)}, f32[768,12,64]{0,2,1:T(8,128)}, ...), condition=%wide.region_7.8_spmd.clone, body=%wide.region_6.7_spmd.clone.sunk | while | flops 1228013568 | bytes 7522923 | solution.py:78
  350.7 28.6 %multiply_convert_fusion.1 = (bf16[768,3072]{1,0:T(8,128)(2,1)S(1)}, f32[768,3072]{1,0:T(8,128)}, f32[768,3072]{1,0:T(8,128)}) fusion(f32[3072]{0:T(1024)S(1)} %copy-done.55, bf16[768,3072]{1,0:T(8,128)(2,1)S(1)} %bitcast.173, f32[768,768]{0,1:T(8,128)S(1)} %get-tuple-element.449, f32[768]{0:T(1024)S(1)} %copy-done.58, f32[768]{0:T(1024)S(1)} %copy-done.42, ...), kind=kOutput, calls=%fused_computation.51 | convolution fusion | flops 3782541312 | bytes 30695424 | tf_op jit(solution)/shard_map/dot_general | solution.py:196
  392.7 12.7 convert_reduce_fusion
  428.1 290.7 %while.41 = (s32[]{:T(128)}, f32[768,12,64]{0,2,1:T(8,128)}, bf16[6,512,12,64]{1,3,2,0:T(8,128)(2,1)}, bf16[6,512,12,64]{1,3,2,0:T(8,128)(2,1)}, bf16[6,512,12,6...) while((s32[]{:T(128)}, f32[768,12,64]{0,2,1:T(8,128)}, ...), condition=%wide.region_16.17_spmd.clone, body=%wide.region_15.16_spmd.clone.sunk | while | flops 3068657664 | bytes 142766832 | solution.py:122
  428.4 10.6 fusion.161
  439.0 10.7 multiply_convert_fusion.13
  464.3 11.9 bitcast_dynamic-update-slice_fusion.5
  476.2 10.6 fusion.161
  486.9 10.7 multiply_convert_fusion.13
  512.7 11.9 bitcast_dynamic-update-slice_fusion.5
  535.3 10.7 multiply_convert_fusion.13
  561.2 11.9 bitcast_dynamic-update-slice_fusion.5
  583.7 10.7 multiply_convert_fusion.13
  609.6 11.9 bitcast_dynamic-update-slice_fusion.5
  621.5 10.6 fusion.161
  632.2 10.7 multiply_convert_fusion.13
  658.1 11.9 bitcast_dynamic-update-slice_fusion.5
  670.0 10.6 fusion.161
  680.6 10.7 multiply_convert_fusion.13
  706.6 11.8 bitcast_dynamic-update-slice_fusion.5
  750.2 10.7 fusion.68
  778.0 50.4 %reduce-scatter.23.cloned.1.call-done = bf16[768,768]{0,1:T(8,128)(2,1)} async-done(((bf16[3072,768]{0,1:T(8,128)(2,1)}), bf16[768,768]{0,1:T(8,128)(2,1)}) %reduce-scatter.23.cloned.1.call-update) | async-done | bytes 1179664 | tf_op jit(solution)/shard_map/reduce_scatter | solution.py:264
  836.9 64.1 %reduce-scatter.35.cloned.1.call-done = f32[96,768]{1,0:T(8,128)} async-done(((f32[768,768]{1,0:T(8,128)}), f32[96,768]{1,0:T(8,128)}) %reduce-scatter.35.cloned.1.call-update) | async-done | bytes 294928 | tf_op jit(solution)/shard_map/reduce_scatter | solution.py:283
  904.4 68.0 %reduce-scatter.27.cloned.1.call-done = f32[96,768]{1,0:T(8,128)} async-done(((f32[768,768]{1,0:T(8,128)}), f32[96,768]{1,0:T(8,128)}) %reduce-scatter.27.cloned.1.call-update) | async-done | bytes 294928 | tf_op jit(solution)/shard_map/reduce_scatter | solution.py:280
  975.9 162.7 %reduce-scatter.33.cloned.1.call-done = f32[384,768]{1,0:T(8,128)} async-done(((f32[3072,768]{1,0:T(8,128)}), f32[384,768]{1,0:T(8,128)}) %reduce-scatter.33.cloned.1.call-update) | async-done | bytes 1179664 | tf_op jit(solution)/shard_map/reduce_scatter | solution.py:282
  1143.1 161.7 %reduce-scatter.29.cloned.1.call-done = f32[96,3072]{1,0:T(8,128)} async-done(((f32[768,3072]{1,0:T(8,128)}), f32[96,3072]{1,0:T(8,128)}) %reduce-scatter.29.cloned.1.call-update) | async-done | bytes 1179664 | tf_op jit(solution)/shard_map/reduce_scatter | solution.py:281
  1307.1 129.6 %reduce-scatter.25.cloned.1.call-done = f32[96,2304]{1,0:T(8,128)} async-done(((f32[768,2304]{1,0:T(8,128)}), f32[96,2304]{1,0:T(8,128)}) %reduce-scatter.25.cloned.1.call-update) | async-done | bytes 884752 | tf_op jit(solution)/shard_map/reduce_scatter | solution.py:279
  1461.4 19.9 %reduce-scatter.39.cloned.1.call-done = bf16[192,96]{1,0:T(8,128)(2,1)} async-done(((bf16[768,96]{1,0:T(8,128)(2,1)}), bf16[192,96]{1,0:T(8,128)(2,1)}) %reduce-scatter.39.cloned.1.call-update) | async-done | bytes 36880
  1499.6 38.7 %all-reduce.9 = (f32[768]{0:T(1024)}, f32[768]{0:T(1024)}, f32[768]{0:T(1024)}, f32[768]{0:T(1024)}, f32[768]{0:T(1024)}, /*index=5*/f32[768]{0:T(1024)}, f32[768]{0:T(1024)}, f32[3072]{0:T(1024)}, f32[768]{0:T(1024)}) all-reduce(f32[768]{0:T(1024)} %get-tuple-element.362, ...), channel_id=5, replica_groups=mesh['grp'=8,'seq'=4] {'grp'}, use_global_device_ids=true, to_apply=%region_22.23.clone | all-reduce | flops 9216 | bytes 73728
  1572.6 92.5 %all-gather.10.cloned.1.call-done = f32[32,150,768]{2,1,0:T(8,128)} async-done(((f32[1,150,768]{2,1,0:T(8,128)}), f32[32,150,768]{2,1,0:T(8,128)}) %all-gather.10.cloned.1.call-update) | async-done | bytes 14745616 | tf_op jit(solution)/shard_map/all_gather | solution.py:215
  (374 shorter events, 427.5 us)
Async XLA Ops:
  7.2 52.1 %all-gather.8.cloned.1.call-start = ((), (), s32[]{:S(2)}) async-start(), calls=%async_computation.13 | async-start | bytes 5898240 | tf_op jit(solution)/shard_map/all_gather | solution.py:183
  19.1 234.1 %all-gather.6.cloned.1.call-start = ((), (), s32[]{:S(2)}) async-start(), calls=%async_computation.12 | async-start | bytes 5898240 | tf_op jit(solution)/shard_map/all_gather | solution.py:184
  19.8 758.2 %reduce-scatter.21.cloned.1.call-start = ((), (), s32[]{:S(2)}) async-start(), calls=%async_computation.14 | async-start | bytes 5898240 | tf_op jit(solution)/shard_map/reduce_scatter | solution.py:261
  26.3 48.2 %copy-start.40 = (f32[150]{0:T(256)}, f32[150]{0:T(256)S(1)}, u32[]{:S(2)}) copy-start(f32[150]{0:T(256)S(1)} %add_rsqrt_fusion.1) | copy-start | bytes 1804
  347.0 32.3 %slice-start = ((s8[4718592]{0:T(1024)(128)(4,1)}), s8[4194304]{0:T(1024)(128)(4,1)S(1)}, s32[]{:S(2)}) async-start(s8[4718592]{0:T(1024)(128)(4,1)} %bitcast.170), calls=%async_computation.27 | async-start | bytes 8388608
  348.3 31.0 %copy-start.7 = (f32[768,768]{0,1:T(8,128)}, f32[768,768]{0,1:T(8,128)S(1)}, u32[]{:S(2)}) copy-start(f32[768,768]{0,1:T(8,128)S(1)} %get-tuple-element.449) | copy-start | bytes 7077892
  348.3 73.9 %copy-start.22 = (f32[768]{0:T(1024)}, f32[768]{0:T(1024)S(1)}, u32[]{:S(2)}) copy-start(f32[768]{0:T(1024)S(1)} %broadcast_multiply_fusion.1) | copy-start | bytes 9220
  350.7 71.6 %copy-start.38 = (f32[768]{0:T(1024)}, f32[768]{0:T(1024)S(1)}, u32[]{:S(2)}) copy-start(f32[768]{0:T(1024)S(1)} %fusion.67) | copy-start | bytes 9220
  350.7 28.7 %slice-start.1 = ((s8[4718592]{0:T(1024)(128)(4,1)}), s8[524288]{0:T(1024)(128)(4,1)S(1)}, s32[]{:S(2)}) async-start(s8[4718592]{0:T(1024)(128)(4,1)} %bitcast.170), calls=%async_computation.28 | async-start | bytes 1048576
  350.7 28.7 %copy-start.57 = (f32[768]{0:T(1024)S(1)}, f32[768]{0:T(1024)}, u32[]{:S(2)}) copy-start(f32[768]{0:T(1024)} %param.39) | copy-start | bytes 9220
  428.3 10.7 copy-start.24
  428.3 10.7 copy-start.25
  439.0 14.4 copy-start.2
  476.2 10.7 copy-start.24
  476.2 10.7 copy-start.25
  486.8 14.4 copy-start.2
  524.6 10.7 copy-start.24
  524.6 10.7 copy-start.25
  535.3 14.4 copy-start.2
  573.1 10.7 copy-start.25
  583.7 14.4 copy-start.2
  621.5 10.7 copy-start.24
  621.5 10.7 copy-start.25
  632.2 14.4 copy-start.2
  670.0 10.7 copy-start.24
  670.0 10.7 copy-start.25
  680.6 14.4 copy-start.2
  730.0 98.5 %reduce-scatter.23.cloned.1.call-start = ((), (), s32[]{:S(2)}) async-start(), calls=%async_computation.15 | async-start | bytes 5898240 | tf_op jit(solution)/shard_map/reduce_scatter | solution.py:264
  741.3 159.7 %reduce-scatter.35.cloned.1.call-start = ((), (), s32[]{:S(2)}) async-start(), calls=%async_computation.21 | async-start | bytes 2654208 | tf_op jit(solution)/shard_map/reduce_scatter | solution.py:283
  745.6 226.9 %reduce-scatter.27.cloned.1.call-start = ((), (), s32[]{:S(2)}) async-start(), calls=%async_computation.17 | async-start | bytes 2654208 | tf_op jit(solution)/shard_map/reduce_scatter | solution.py:280
  749.9 388.7 %reduce-scatter.33.cloned.1.call-start = ((), (), s32[]{:S(2)}) async-start(), calls=%async_computation.20 | async-start | bytes 10616832 | tf_op jit(solution)/shard_map/reduce_scatter | solution.py:282
  760.9 544.0 %reduce-scatter.29.cloned.1.call-start = ((), (), s32[]{:S(2)}) async-start(), calls=%async_computation.18 | async-start | bytes 10616832 | tf_op jit(solution)/shard_map/reduce_scatter | solution.py:281
  772.2 56.2 %copy-start.21 = (f32[768]{0:T(1024)S(1)}, f32[768]{0:T(1024)}, u32[]{:S(2)}) copy-start(f32[768]{0:T(1024)} %copy-done.20) | copy-start | bytes 9220
  772.2 56.2 %copy-start.30 = (f32[768]{0:T(1024)S(1)}, f32[768]{0:T(1024)}, u32[]{:S(2)}) copy-start(f32[768]{0:T(1024)} %copy-done.29) | copy-start | bytes 9220
  772.2 56.2 %copy-start.34 = (f32[768]{0:T(1024)S(1)}, f32[768]{0:T(1024)}, u32[]{:S(2)}) copy-start(f32[768]{0:T(1024)} %param.27) | copy-start | bytes 9220
  772.2 56.2 %copy-start.61 = (f32[768]{0:T(1024)S(1)}, f32[768]{0:T(1024)}, u32[]{:S(2)}) copy-start(f32[768]{0:T(1024)} %param.28) | copy-start | bytes 9220
  772.3 664.4 %reduce-scatter.25.cloned.1.call-start = ((), (), s32[]{:S(2)}) async-start(), calls=%async_computation.16 | async-start | bytes 7962624 | tf_op jit(solution)/shard_map/reduce_scatter | solution.py:279
  836.8 621.6 %reduce-scatter.43.cloned.1.call-start = ((), (), s32[]{:S(2)}) async-start(), calls=%async_computation.26 | async-start | bytes 245760
  904.4 577.0 %reduce-scatter.39.cloned.1.call-start = ((), (), s32[]{:S(2)}) async-start(), calls=%async_computation.24 | async-start | bytes 245760
  975.9 588.3 %reduce-scatter.41.cloned.1.call-start = ((), (), s32[]{:S(2)}) async-start(), calls=%async_computation.25 | async-start | bytes 737280
  1143.0 298.1 %copy-start.27 = (f32[768]{0:T(1024)S(1)}, f32[768]{0:T(1024)}, u32[]{:S(2)}) copy-start(f32[768]{0:T(1024)} %copy-done.26) | copy-start | bytes 9220
  1143.0 298.1 %copy-start.28 = (f32[768]{0:T(1024)S(1)}, f32[768]{0:T(1024)}, u32[]{:S(2)}) copy-start(f32[768]{0:T(1024)} %get-tuple-element.447) | copy-start | bytes 9220
  1143.0 424.6 %reduce-scatter.31.cloned.1.call-start = ((), (), s32[]{:S(2)}) async-start(), calls=%async_computation.19 | async-start | bytes 737280 | tf_op jit(solution)/shard_map/reduce_scatter | solution.py:301
  1307.0 262.3 %reduce-scatter.37.cloned.1.call-start = ((), (), s32[]{:S(2)}) async-start(), calls=%async_computation.23 | async-start | bytes 737280
  1440.8 224.3 %all-gather.10.cloned.1.call-start = ((), (), s32[]{:S(2)}) async-start(), calls=%async_computation.22 | async-start | bytes 15409152 | tf_op jit(solution)/shard_map/all_gather | solution.py:215
  1497.9 51.2 %copy-start.36 = (f32[768]{0:T(1024)S(1)}, f32[768]{0:T(1024)}, u32[]{:S(2)}) copy-start(f32[768]{0:T(1024)} %param.27) | copy-start | bytes 9220
  1572.6 100.8 %copy-start.46 = (f32[150]{0:T(256)S(1)}, f32[150]{0:T(256)}, u32[]{:S(2)}) copy-start(f32[150]{0:T(256)} %copy-done.45) | copy-start | bytes 1804
  1572.6 100.8 %copy-start.41 = (f32[150]{0:T(256)S(1)}, f32[150]{0:T(256)}, u32[]{:S(2)}) copy-start(f32[150]{0:T(256)} %copy-done.40) | copy-start | bytes 1804
  (56 other events, 180.7 us)
Sparse Core Ops, SparseCore 0:
  19.2 40.1 all-gather.7
  60.9 37.4 all-gather.5
  730.1 47.8 reduce-scatter.20
  780.5 47.8 reduce-scatter.22
  831.8 69.1 reduce-scatter.34
  904.3 68.0 reduce-scatter.26
  976.1 162.5 reduce-scatter.32
  1142.2 162.5 reduce-scatter.28
  1308.5 128.0 reduce-scatter.24
  1439.7 18.7 reduce-scatter.42
  1461.6 19.6 reduce-scatter.38
  1483.9 22.0 reduce-scatter.40
  1508.7 22.0 reduce-scatter.30
  1533.3 22.0 reduce-scatter.36
  1558.5 106.5 all-gather.9
